TPU v7x, 32 devices: a whole 2x2x4 slice. The times are simulated.
32 devices in a mesh: grid: 8 (over z, x), freq: 4 (over y, core).
Axes of the slice: x: 2, y: 2, z: 4, core: 2. Of those that a mesh axis runs over, the one named last changes fastest.
Arguments:
- traces: bfloat16 [32, 8, 16, 2048], P(('grid', 'freq')), may hold values from -6 to 6
- bins: int32 [32, 8, 16], P(('grid', 'freq')), may hold values from 0 to 12287, as said below
- live: int32 [32, 8, 16], P(('grid', 'freq')), may hold values 0 or 1
- probe: float32 [64, 2, 24], replicated, may hold values from -0.5 to 0.5
Outputs:
- reconstructed: float32 [96, 16, 64, 512], P('grid', None, None, 'freq')
Inputs may be any that keep to these rules, and one draw needn't show every extreme that they name: Within one destination tile the bins of all sources' slots are distinct; in each tile some slot names cell 0 and some slot names cell 12288 - 1.
All inputs are finite; a program needn't handle non-finite values. No bound on the sum of `live` on one device may be relied on, other than what follows from the above.
Results may differ from a plain program's by a relative error of at most 0.0052.
Values may be sent and summed in bfloat16 or wider, within the bound.
No kernel may reach another device: no remote copies, remote signals or barrier semaphores. Data moves between devices by JAX's collectives and lax.ppermute only.
A program may use at most 128 MiB of HBM per device.

v0:
```python
import functools
import math

import jax
import jax.numpy as jnp
from jax import lax
from jax.experimental import pallas as pl
from jax.experimental.pallas import tpu as pltpu
from jax.sharding import PartitionSpec as P

FDEV = 64
FIRST = 8
PX = 16
MY = 16
HC = 64
MARGIN = 2
OWNX = 12
RANK = 24
SPAN = 5
OWN_ROWS = OWNX * MY
RIM = MARGIN * MY
ROWS = PX * MY
COLS = 2 * FDEV
JG = 8
RP = 32
BLOCK_SRC = 32
DEAD = 255.0

f32 = jnp.float32
bf16 = jnp.bfloat16


def dot(a, b):
    return jnp.dot(a, b, preferred_element_type=f32)


def split(x):
    high = x.astype(bf16)
    return high, (x - high.astype(f32)).astype(bf16)


def iota(shape, dim):
    return lax.broadcasted_iota(jnp.int32, shape, dim)


def phase(times, columns, length, quarter):
    k = FIRST + columns // COLS * FDEV + columns % FDEV
    turns = ((times * k) & (length - 1)).astype(f32)
    angle = turns * (2.0 * math.pi / length)
    if quarter:
        angle = angle + (columns // FDEV % 2).astype(f32) * (0.5 * math.pi)
    return jnp.cos(angle), jnp.sin(angle)


def spectra_kernel(traces_ref, marks_ref, out_ref, table_ref):
    length, width = table_ref.shape
    tiles, bands = out_ref.shape[:2]
    slots = traces_ref.shape[0] // tiles
    coarse = length // 64
    column = iota((1, width), 1)
    col = lambda n: column + jnp.zeros((n, 1), jnp.int32)
    c1, s1 = phase(iota((coarse, width), 0) * 64, col(coarse), length, False)
    c2, s2 = phase(iota((8, width), 0) * 8, col(8), length, False)
    c3, s3 = phase(iota((8, width), 0), col(8), length, True)
    scale = 1.0 / math.sqrt(length)
    c3, s3 = c3 * scale, s3 * scale
    fine_c = jnp.concatenate([c2[i : i + 1] * c3 - s2[i : i + 1] * s3 for i in range(8)], 0)
    fine_s = jnp.concatenate([s2[i : i + 1] * c3 + c2[i : i + 1] * s3 for i in range(8)], 0)
    for i in range(coarse):
        block = c1[i : i + 1] * fine_c - s1[i : i + 1] * fine_s
        table_ref[64 * i : 64 * i + 64, :] = block.astype(bf16)
    spectra = dot(traces_ref[...], table_ref[...]).astype(bf16)
    nothing = jnp.zeros((slots, COLS), bf16)
    for band in range(bands):
        piece = spectra[:, band * COLS : (band + 1) * COLS]
        for tile in range(tiles):
            for t in range(SPAN):
                source = tile - 2 + t
                there = 0 <= source < tiles
                out_ref[tile, band, t * slots : (t + 1) * slots, :] = (
                    piece[source * slots : (source + 1) * slots] if there else nothing
                )
            out_ref[tile, band, SPAN * slots : SPAN * slots + 2, :] = marks_ref[tile]


def patch_kernel(
    tiles,
    slots,
    arrived_ref,
    probe_ref,
    out_ref,
    st_ref,
    pp_ref,
    own_ref,
    gram_ref,
    sem,
):
    sources = arrived_ref.shape[0]
    per = min(BLOCK_SRC, sources)
    n = per * slots
    chunks = sources // per
    nb = SPAN * chunks
    pl.run_scoped(
        functools.partial(project, slots, arrived_ref, probe_ref, st_ref, pp_ref, own_ref, gram_ref),
        pltpu.VMEM((nb, COLS, n), f32),
        pltpu.VMEM((nb, 2 * RANK, n), f32),
        pltpu.VMEM((nb, ROWS, n), bf16),
        pltpu.VMEM((nb, n, ROWS), bf16),
        pltpu.VMEM((nb, n, 3 * HC), bf16),
    )
    invert_grams(gram_ref)
    pl.run_scoped(
        functools.partial(write, tiles, own_ref, pp_ref, gram_ref, out_ref, sem),
        pltpu.VMEM((FDEV, OWN_ROWS, COLS), f32),
        pltpu.VMEM((OWN_ROWS, HC, COLS), f32),
    )


def over(chunks, body, carry):
    if chunks == 1:
        return body(0, carry)
    return lax.fori_loop(0, chunks, body, carry)


def project(
    slots,
    arrived_ref,
    probe_ref,
    st_ref,
    pp_ref,
    own_ref,
    gram_ref,
    vt_ref,
    wt_ref,
    ohm_ref,
    ohmt_ref,
    ohht_ref,
):
    sources = arrived_ref.shape[0]
    per = min(BLOCK_SRC, sources)
    n = per * slots
    chunks = sources // per
    group_of = (0, 0, 1, 2, 2)

    lane_src = (iota((per, n), 1) // slots == iota((per, n), 0)).astype(f32)
    for t in range(SPAN):

        def prepare(chunk, carry, t=t):
            b = t * chunks + chunk
            pick = (iota((COLS, n), 0) == t * slots + iota((COLS, n), 1) % slots).astype(f32).astype(bf16)
            marks = arrived_ref[pl.ds(chunk * per, per), SPAN * slots : SPAN * slots + 2, :].astype(f32)
            rows = []
            for i in range(2):
                spread = dot(marks[:, i, :].astype(bf16), pick)
                rows.append(jnp.sum(spread * lane_src, 0, keepdims=True))
            m, h = rows
            good = m < OWN_ROWS
            low, high = m < RIM, m >= OWN_ROWS - RIM
            if t == 0:
                inside = [good & high, None, None]
                place = jnp.where(good & high, m - (OWN_ROWS - RIM), DEAD + 1)
            elif t == 1:
                inside = [good, good & high, None]
                place = jnp.where(good, m + RIM, DEAD + 1)
            elif t == 2:
                inside = [good & low, good, good & high]
                place = jnp.where(good, m, DEAD + 1)
            elif t == 3:
                inside = [None, good & low, good]
                place = jnp.where(good, m, DEAD + 1)
            else:
                inside = [None, None, good & low]
                place = jnp.where(good & low, m + OWN_ROWS, DEAD + 1)
            offset = [
                jnp.full_like(h, -1.0) if ok is None else jnp.where(ok, h, -1.0) for ok in inside
            ]
            marks8 = jnp.concatenate([place] + offset + [h, h, h, h], 0)
            marks_t = marks8.T
            ohm_ref[b] = (iota((ROWS, n), 0).astype(f32) == place).astype(f32).astype(bf16)
            ohmt_ref[b] = (iota((n, ROWS), 1).astype(f32) == marks_t[:, 0:1]).astype(f32).astype(bf16)
            ohht_ref[b] = jnp.concatenate(
                [
                    (iota((n, HC), 1).astype(f32) == marks_t[:, 1 + p : 2 + p]).astype(f32)
                    for p in range(3)
                ],
                1,
            ).astype(bf16)
            ohh = (iota((HC, n), 0).astype(f32) == h).astype(f32).astype(bf16)
            p_high, p_low = split(probe_ref[...])
            wt_ref[b] = dot(p_high, ohh) + dot(p_low, ohh)
            values = arrived_ref[pl.ds(chunk * per, per), t * slots : (t + 1) * slots, :].reshape(n, COLS)
            vt_ref[b] = values.astype(f32).T
            return carry

        over(chunks, prepare, 0)

    st_ref[...] = jnp.zeros_like(st_ref)
    pp_ref[...] = jnp.zeros_like(pp_ref)
    lane = iota((RANK * JG, ROWS), 1)

    def step(g, carry):
        sketch = [None, None, None]
        for t in range(SPAN):

            def gather(chunk, total, t=t):
                b = t * chunks + chunk
                w = wt_ref[b]
                u = []
                for j in range(JG):
                    re = vt_ref[b, pl.ds(g * JG + j, 1), :]
                    im = vt_ref[b, pl.ds(FDEV + g * JG + j, 1), :]
                    u.append(w[:RANK] * re + w[RANK:] * im)
                part = dot(jnp.concatenate(u, 0).astype(bf16), ohmt_ref[b])
                return part if total is None else total + part

            k = group_of[t]
            first = None if chunks == 1 else jnp.zeros((RANK * JG, ROWS), f32)
            sketch[k] = over(chunks, gather, first if sketch[k] is None else sketch[k])
        left, own, right = sketch
        sk = [x.astype(bf16) for x in sketch]
        proj = None if chunks == 1 else jnp.zeros((2 * RANK * JG, 3 * HC), f32)
        for t in range(SPAN):

            def scatter(chunk, total, t=t):
                b = t * chunks + chunk
                at = dot(sk[group_of[t]], ohm_ref[b])
                z = []
                for c in range(2):
                    for j in range(JG):
                        v = vt_ref[b, pl.ds(c * FDEV + g * JG + j, 1), :]
                        z.append(at[j * RANK : (j + 1) * RANK] * v)
                part = dot(jnp.concatenate(z, 0).astype(bf16), ohht_ref[b])
                return part if total is None else total + part

            proj = over(chunks, scatter, proj)
        full_left = jnp.where(lane < ROWS - RIM, left, pltpu.roll(own, ROWS - RIM, 1))
        full_right = jnp.where(lane < ROWS - RIM, right, pltpu.roll(own, ROWS - OWN_ROWS, 1))
        full_own = jnp.where(
            lane < OWN_ROWS,
            own,
            jnp.where(lane < OWN_ROWS + RIM, left, pltpu.roll(right, ROWS - RIM, 1)),
        )
        half = RANK * JG
        re, im = proj[:half], proj[half:]
        lo = iota((half, COLS), 1) < HC
        parts = [
            jnp.where(lo, re[:, :COLS], pltpu.roll(im[:, :COLS], HC, 1)),
            jnp.where(lo, pltpu.roll(re[:, :COLS], HC, 1), im[:, :COLS]),
            jnp.where(
                lo,
                jnp.concatenate([re[:, COLS:], re[:, COLS:]], 1),
                jnp.concatenate([im[:, COLS:], im[:, COLS:]], 1),
            ),
        ]
        for p, whole in enumerate((full_left, full_own, full_right)):
            st_ref[p, :, :RANK, :] = whole.reshape(JG, RANK, ROWS)
            pp_ref[p, pl.ds(g * JG, JG), :RANK, :] = parts[p].reshape(JG, RANK, COLS)
            pad = st_ref[p].reshape(JG * RP, ROWS).astype(bf16)
            if p == 1:
                own_ref[g] = st_ref[p].reshape(JG * RP, ROWS).T[:OWN_ROWS].astype(bf16)
            gram = lax.dot_general(pad, pad, (((1,), (1,)), ((), ())), preferred_element_type=f32)
            for q2 in range(2):
                lanes = iota((RANK, 4 * RP), 1) // RP
                acc = jnp.zeros((RANK, 4 * RP), f32)
                for q in range(4):
                    at = (q2 * 4 + q) * RP
                    piece = gram[at : at + RANK, q2 * 4 * RP : (q2 + 1) * 4 * RP]
                    acc = jnp.where(lanes == q, piece, acc)
                gram_ref[p, 2 * g + q2] = acc
        return carry

    lax.fori_loop(0, FDEV // JG, step, 0)


def invert_grams(gram_ref):
    count = FDEV // 4
    batch = 8
    wide = 4 * RP
    lane3 = iota((batch, RANK, wide), 2) % RP
    row3 = iota((batch, RANK, wide), 1)
    lane1 = iota((batch, 1, wide), 2) % RP
    base = iota((batch * RANK, wide), 1) // RP * RP
    same = (iota((wide, wide), 0) // RP == iota((wide, wide), 1) // RP).astype(f32)

    def invert(i, carry):
        p, c = i // (count // batch), i % (count // batch)
        a = gram_ref[p, pl.ds(c * batch, batch)]
        diag = jnp.sum(jnp.where(lane3 == row3, a, 0.0), 1)
        trace = jnp.dot(
            diag, same, preferred_element_type=f32, precision=lax.Precision.HIGHEST
        )
        ridge = 0.01 * trace / RANK + 1e-06
        a = a + jnp.where(lane3 == row3, ridge[:, None, :], 0.0)
        for k in range(RANK):
            flat = a.reshape(batch * RANK, wide)
            column = jnp.take_along_axis(flat, base + k, axis=1).reshape(batch, RANK, wide)
            scale = 1.0 / column[:, k : k + 1]
            pivot = jnp.where(lane1 == k, scale, a[:, k : k + 1] * scale)
            rest = jnp.where(lane3 == k, 0.0, a) - column * pivot
            a = jnp.where(row3 == k, pivot, rest)
        gram_ref[p, pl.ds(c * batch, batch)] = a
        return carry

    lax.fori_loop(0, 3 * count // batch, invert, 0)


def write(tiles, own_ref, pp_ref, gram_ref, out_ref, sem, freq_ref, cells_ref):
    count = FDEV // 4
    wide = 4 * RP
    here = lax.axis_index("grid")
    has_left = (here > 0).astype(f32)
    has_right = (here < tiles - 1).astype(f32)
    edge = iota((RIM, 1), 0) < MY
    taper_first = jnp.where(edge, 0.6, 0.8)
    taper_last = jnp.where(edge, 0.8, 0.6)
    left_w = jnp.where(edge, 0.4, 0.2) * has_left
    right_w = jnp.where(edge, 0.2, 0.4) * has_right

    def rebuild(i, carry):
        rows = own_ref[i // 2, :, pl.ds(pl.multiple_of(i % 2 * wide, wide), wide)]
        weights = []
        for p in range(3):
            inverse = gram_ref[p, i]
            lanes = iota((RANK, wide), 1) // RP
            zero = jnp.zeros((RP - RANK, wide), f32)
            diag = []
            for q in range(4):
                diag += [jnp.where(lanes == q, inverse, 0.0), zero]
            b_high, b_low = split(jnp.concatenate(diag, 0))
            p_high, p_low = split(pp_ref[p, pl.ds(i * 4, 4)].reshape(wide, COLS))
            coeff = dot(b_high, p_high) + dot(b_high, p_low) + dot(b_low, p_high)
            weights.append(coeff)
        quarter = iota((wide, COLS), 0) // RP
        for a in range(2):
            w = [
                jnp.concatenate([jnp.where(quarter == 2 * a + e, x, 0.0) for e in range(2)], 1).astype(bf16)
                for x in weights
            ]
            mid = dot(rows, w[1])
            first = mid[:RIM] * taper_first + dot(rows[:RIM], w[0]) * left_w
            last = mid[OWN_ROWS - RIM :] * taper_last + dot(rows[OWN_ROWS - RIM :], w[2]) * right_w
            full = jnp.concatenate([first, mid[RIM : OWN_ROWS - RIM], last], 0)
            for e in range(2):
                freq_ref[i * 4 + 2 * a + e] = full[:, e * COLS : (e + 1) * COLS]
        return carry

    lax.fori_loop(0, count, rebuild, 0)

    unroll = 4
    half_lane = iota((HC, COLS), 1) < FDEV

    def turn(i, carry):
        for q in range(unroll):
            m = (i * unroll + q) * 2
            both = jnp.concatenate([freq_ref[:, m, :], freq_ref[:, m + 1, :]], 0)
            flip = both.T
            re, im = flip[:HC], flip[HC:]
            cells_ref[m] = jnp.where(half_lane, re, pltpu.roll(im, FDEV, 1))
            cells_ref[m + 1] = jnp.where(half_lane, pltpu.roll(re, FDEV, 1), im)
        return carry

    pieces = 6
    size = OWN_ROWS // pieces
    copies = []
    for k in range(pieces):
        per_piece = size // (2 * unroll)
        lax.fori_loop(k * per_piece, (k + 1) * per_piece, turn, 0)
        copy = pltpu.make_async_copy(
            cells_ref.at[pl.ds(k * size, size)], out_ref.at[pl.ds(k * size, size)], sem.at[k]
        )
        copy.start()
        copies.append(copy)
    for copy in copies:
        copy.wait()


def per_device(traces, bins, live, probe):
    tiles = lax.axis_size("grid")
    bands = lax.axis_size("freq")
    slots, length = traces.shape[2:]
    sources = tiles * bands
    used = SPAN * slots

    on = live[0] == 1
    mark = jnp.stack(
        [jnp.where(on, bins[0] // HC, int(DEAD)), jnp.where(on, bins[0] % HC, 0)], 1
    ).astype(bf16)
    mark = jnp.pad(mark, ((2, 2), (0, 0), (0, 0)), constant_values=DEAD)
    marks = jnp.concatenate([mark[t : t + tiles] for t in range(SPAN)], 2)
    marks = jnp.pad(marks, ((0, 0), (0, 0), (0, COLS - used)))

    vmem = pl.BlockSpec(memory_space=pltpu.VMEM)
    sent = pl.pallas_call(
        spectra_kernel,
        out_shape=jax.ShapeDtypeStruct((tiles, bands, used + 2, COLS), bf16),
        in_specs=[vmem, vmem],
        out_specs=vmem,
        scratch_shapes=[pltpu.VMEM((length, COLS * bands), bf16)],
        compiler_params=pltpu.CompilerParams(vmem_limit_bytes=48 * 2**20),
        name="spectra",
    )(traces.reshape(tiles * slots, length), marks)

    arrived = lax.all_to_all(
        sent.reshape(sources, used + 2, COLS), ("grid", "freq"), 0, 0, tiled=True
    )

    out = pl.pallas_call(
        functools.partial(patch_kernel, tiles, slots),
        out_shape=jax.ShapeDtypeStruct((OWN_ROWS, HC, COLS), f32),
        in_specs=[vmem, vmem],
        out_specs=pl.BlockSpec(memory_space=pl.ANY),
        scratch_shapes=[
            pltpu.VMEM((3, JG, RP, ROWS), f32),
            pltpu.VMEM((3, FDEV, RP, COLS), f32),
            pltpu.VMEM((FDEV // JG, OWN_ROWS, JG * RP), bf16),
            pltpu.VMEM((3, FDEV // 4, RANK, 4 * RP), f32),
            pltpu.SemaphoreType.DMA((6,)),
        ],
        compiler_params=pltpu.CompilerParams(vmem_limit_bytes=60 * 2**20),
        name="patches",
    )(arrived, jnp.transpose(probe, (1, 2, 0)).reshape(2 * RANK, HC))
    return out.reshape(OWNX, MY, HC, COLS)


def solution(mesh):
    placed = (
        P(("grid", "freq"), None, None, None),
        P(("grid", "freq"), None, None),
        P(("grid", "freq"), None, None),
        P(),
    )
    return jax.shard_map(
        per_device,
        mesh=mesh,
        in_specs=placed,
        out_specs=P("grid", None, None, "freq"),
        check_vma=False,
    )
```

profile of v0, /device:TPU:0, one launch (start us, length us, event | category | flops | bytes accessed | tf_op | source)
XLA Modules:
  0.0 80.5 jit_solution(10089400025551645024)
XLA Ops:
  0.0 0.7 compare_bitcast_fusion
  0.7 0.7 fusion
  1.5 0.1 concatenate.3
  1.6 0.0 copy-start
  1.6 1.0 %copy-done = bf16[1,8,16,2048]{3,2,1,0:T(8,128)(2,1)S(1)} copy-done((bf16[1,8,16,2048]{3,2,1,0:T(8,128)(2,1)S(1)}, bf16[1,8,16,2048]{3,2,1,0:T(8,128)(2,1)}, u32[]{:S(2)}) %copy-start) | copy-done | bytes 524312
  2.7 1.2 %spectra.1 = bf16[8,4,82,128]{3,2,1,0:T(8,128)(2,1)S(1)} custom-call(bf16[128,2048]{1,0:T(8,128)(2,1)S(1)} %bitcast.12, bf16[8,2,128]{2,1,0:T(2,128)(2,1)S(1)} %pad.9.marks_ref), custom_call_target="tpu_custom_call" | custom-call | tf_op jit(solution)/shard_map/spectra/pallas_call | solution.py:393
  3.9 26.4 %all_to_all.5.arrived_ref = bf16[32,82,128]{2,1,0:T(8,128)(2,1)} all-to-all(bf16[32,82,128]{2,1,0:T(8,128)(2,1)S(1)} %bitcast.11), channel_id=1, replica_groups=mesh['grid'=8,'freq'=4] {'grid','freq'}, dimensions={0} | all-to-all | bytes 1343488 | tf_op jit(solution)/shard_map/all_to_all | solution.py:403
  30.3 50.2 %patches.1 = f32[192,64,128]{2,1,0:T(8,128)} custom-call(bf16[32,82,128]{2,1,0:T(8,128)(2,1)} %all_to_all.5.arrived_ref, f32[48,64]{1,0:T(8,128)} %bitcast.13), custom_call_target="tpu_custom_call" | custom-call | tf_op jit(solution)/shard_map/patches/pallas_call | solution.py:407
  (4 shorter events, 0.1 us)
Async XLA Ops:
  1.6 1.0 %copy-start = (bf16[1,8,16,2048]{3,2,1,0:T(8,128)(2,1)S(1)}, bf16[1,8,16,2048]{3,2,1,0:T(8,128)(2,1)}, u32[]{:S(2)}) copy-start(bf16[1,8,16,2048]{3,2,1,0:T(8,128)(2,1)} %param.4) | copy-start | bytes 1572868
where the time goes:
time: 80.8 us; the launch traced here: 80.5 us
  Pallas kernels  51.4 us (64%)
  blocking collectives  26.4 us (33%)
  other arithmetic  1.44 us (2%)
  local copies, waits for them, and re-layouts  1.18 us (1%)
    pallas_call x1, Pallas kernels, per_device(): pl.pallas_call(functools.partial(patch_kernel, tiles, slots), out_shape=j...  50.2 us
    all_to_all x1, blocking collectives, per_device(): lax.all_to_all(sent.reshape(sources, used + 2, COLS), ('grid', 'freq'), 0...  26.4 us

commit v1 on v0

--- a/solution.py
+++ b/solution.py
@@ -99,7 +99,8 @@
     per = min(BLOCK_SRC, sources)
     n = per * slots
     chunks = sources // per
-    nb = SPAN * chunks
+    side = chunks + rim_blocks(chunks, n)
+    nb = chunks + 2 * side
     pl.run_scoped(
         functools.partial(project, slots, arrived_ref, probe_ref, st_ref, pp_ref, own_ref, gram_ref),
         pltpu.VMEM((nb, COLS, n), f32),
@@ -107,6 +108,8 @@
         pltpu.VMEM((nb, ROWS, n), bf16),
         pltpu.VMEM((nb, n, ROWS), bf16),
         pltpu.VMEM((nb, n, 3 * HC), bf16),
+        pltpu.VMEM((SPAN * chunks, 1, n), f32),
+        pltpu.VMEM((SPAN * chunks, 8, n), f32),
     )
     invert_grams(gram_ref)
     pl.run_scoped(
@@ -114,6 +117,10 @@
         pltpu.VMEM((FDEV, OWN_ROWS, COLS), f32),
         pltpu.VMEM((OWN_ROWS, HC, COLS), f32),
     )
+
+
+def rim_blocks(chunks, n):
+    return (min(RIM * HC, chunks * n) + n - 1) // n
 
 
 def over(chunks, body, carry):
@@ -135,104 +142,143 @@
     ohm_ref,
     ohmt_ref,
     ohht_ref,
+    rank_ref,
+    fact_ref,
 ):
     sources = arrived_ref.shape[0]
     per = min(BLOCK_SRC, sources)
     n = per * slots
     chunks = sources // per
-    group_of = (0, 0, 1, 2, 2)
+    members = ((0, 1), (2,), (3, 4))
+    side = chunks + rim_blocks(chunks, n)
+    first = (0, side, side + chunks)
 
     lane_src = (iota((per, n), 1) // slots == iota((per, n), 0)).astype(f32)
-    for t in range(SPAN):
-
-        def prepare(chunk, carry, t=t):
-            b = t * chunks + chunk
-            pick = (iota((COLS, n), 0) == t * slots + iota((COLS, n), 1) % slots).astype(f32).astype(bf16)
-            marks = arrived_ref[pl.ds(chunk * per, per), SPAN * slots : SPAN * slots + 2, :].astype(f32)
+    before = (iota((n, n), 0) < iota((n, n), 1)).astype(f32).astype(bf16)
+
+    def locate(chunk, totals):
+        totals = list(totals)
+        marks = arrived_ref[pl.ds(chunk * per, per), SPAN * slots : SPAN * slots + 2, :].astype(f32)
+        facts, used = [], []
+        for t in range(SPAN):
+            pick = (iota((COLS, n), 0) == t * slots + iota((COLS, n), 1) % slots).astype(f32)
+            pick = pick.astype(bf16)
             rows = []
             for i in range(2):
                 spread = dot(marks[:, i, :].astype(bf16), pick)
                 rows.append(jnp.sum(spread * lane_src, 0, keepdims=True))
             m, h = rows
             good = m < OWN_ROWS
-            low, high = m < RIM, m >= OWN_ROWS - RIM
-            if t == 0:
-                inside = [good & high, None, None]
-                place = jnp.where(good & high, m - (OWN_ROWS - RIM), DEAD + 1)
-            elif t == 1:
-                inside = [good, good & high, None]
-                place = jnp.where(good, m + RIM, DEAD + 1)
-            elif t == 2:
-                inside = [good & low, good, good & high]
-                place = jnp.where(good, m, DEAD + 1)
-            elif t == 3:
-                inside = [None, good & low, good]
-                place = jnp.where(good, m, DEAD + 1)
-            else:
-                inside = [None, None, good & low]
-                place = jnp.where(good & low, m + OWN_ROWS, DEAD + 1)
-            offset = [
-                jnp.full_like(h, -1.0) if ok is None else jnp.where(ok, h, -1.0) for ok in inside
-            ]
-            marks8 = jnp.concatenate([place] + offset + [h, h, h, h], 0)
-            marks_t = marks8.T
-            ohm_ref[b] = (iota((ROWS, n), 0).astype(f32) == place).astype(f32).astype(bf16)
-            ohmt_ref[b] = (iota((n, ROWS), 1).astype(f32) == marks_t[:, 0:1]).astype(f32).astype(bf16)
-            ohht_ref[b] = jnp.concatenate(
-                [
-                    (iota((n, HC), 1).astype(f32) == marks_t[:, 1 + p : 2 + p]).astype(f32)
-                    for p in range(3)
-                ],
-                1,
-            ).astype(bf16)
-            ohh = (iota((HC, n), 0).astype(f32) == h).astype(f32).astype(bf16)
-            p_high, p_low = split(probe_ref[...])
-            wt_ref[b] = dot(p_high, ohh) + dot(p_low, ohh)
-            values = arrived_ref[pl.ds(chunk * per, per), t * slots : (t + 1) * slots, :].reshape(n, COLS)
-            vt_ref[b] = values.astype(f32).T
+            low, high = m < RIM, good & (m >= OWN_ROWS - RIM)
+            keep = (high, good, good, good, low)[t]
+            shift = (RIM - OWN_ROWS, RIM, 0, 0, OWN_ROWS)[t]
+            inside = (
+                (high, None, None),
+                (good, high, None),
+                (low, good, high),
+                (None, low, good),
+                (None, None, low),
+            )[t]
+            fact = [jnp.where(keep, m + shift + 1.0, 0.0), jnp.where(keep, h + 1.0, 0.0)]
+            for ok in inside:
+                fact.append(jnp.zeros_like(h) if ok is None else jnp.where(ok, h + 1.0, 0.0))
+            facts.append(jnp.concatenate(fact + [jnp.zeros((3, n), f32)], 0))
+            used.append(keep.astype(f32))
+        use = jnp.concatenate(used + [jnp.zeros((8 - SPAN, n), f32)], 0)
+        ranks = dot(use.astype(bf16), before)
+        sums = jnp.sum(use, 1, keepdims=True)
+        for k in range(3):
+            for t in members[k]:
+                rank = ranks[t : t + 1] + totals[k]
+                rank_ref[t * chunks + chunk] = jnp.where(use[t : t + 1] > 0.5, rank, -1.0)
+                fact_ref[t * chunks + chunk] = facts[t]
+                totals[k] = totals[k] + sums[t : t + 1]
+        return tuple(totals)
+
+    zero = jnp.zeros((1, 1), f32)
+    totals = over(chunks, locate, (zero, zero, zero))
+    counts = [jnp.max(x).astype(jnp.int32) for x in totals]
+    filled = [(c + (n - 1)) // n for c in counts]
+
+    p_high, p_low = split(probe_ref[...])
+
+    def pack(k, q):
+        def gather(chunk, total, t):
+            b = t * chunks + chunk
+            wanted = iota((n, n), 0).astype(f32) + (q * n).astype(f32)
+            chosen = (wanted == rank_ref[b]).astype(f32).astype(bf16)
+            values = arrived_ref[pl.ds(chunk * per, per), t * slots : (t + 1) * slots, :]
+            fact = jnp.concatenate([fact_ref[b], jnp.zeros((COLS - 8, n), f32)], 0).T
+            both = jnp.concatenate([values.reshape(n, COLS), fact.astype(bf16)], 1)
+            part = dot(chosen, both)
+            return part if total is None else total + part
+
+        total = None if chunks == 1 else jnp.zeros((n, 2 * COLS), f32)
+        for t in members[k]:
+            total = over(chunks, functools.partial(gather, t=t), total)
+        flip = total.T
+        b = first[k] + q
+        vt_ref[b] = flip[:COLS]
+        row, h = flip[COLS : COLS + 1] - 1.0, flip[COLS + 1 : COLS + 2] - 1.0
+        column = total[:, COLS : COLS + 8] - 1.0
+        ohm_ref[b] = (iota((ROWS, n), 0).astype(f32) == row).astype(f32).astype(bf16)
+        ohmt_ref[b] = (iota((n, ROWS), 1).astype(f32) == column[:, 0:1]).astype(f32).astype(bf16)
+        ohht_ref[b] = jnp.concatenate(
+            [
+                (iota((n, HC), 1).astype(f32) == column[:, 2 + p : 3 + p]).astype(f32)
+                for p in range(3)
+            ],
+            1,
+        ).astype(bf16)
+        ohh = (iota((HC, n), 0).astype(f32) == h).astype(f32).astype(bf16)
+        wt_ref[b] = dot(p_high, ohh) + dot(p_low, ohh)
+
+    for k in range(3):
+        pack(k, jnp.int32(0))
+
+        def more(q, carry, k=k):
+            pack(k, q)
             return carry
 
-        over(chunks, prepare, 0)
-
-    st_ref[...] = jnp.zeros_like(st_ref)
-    pp_ref[...] = jnp.zeros_like(pp_ref)
+        lax.fori_loop(1, filled[k], more, 0)
+
+    st_ref[:, :, RANK:, :] = jnp.zeros((3, JG, RP - RANK, ROWS), f32)
+    pp_ref[:, :, RANK:, :] = jnp.zeros((3, FDEV, RP - RANK, COLS), f32)
     lane = iota((RANK * JG, ROWS), 1)
 
-    def step(g, carry):
-        sketch = [None, None, None]
-        for t in range(SPAN):
-
-            def gather(chunk, total, t=t):
-                b = t * chunks + chunk
-                w = wt_ref[b]
-                u = []
+    def step(g, carry, short):
+        def sketch_of(b):
+            w = wt_ref[b]
+            u = []
+            for j in range(JG):
+                re = vt_ref[b, pl.ds(g * JG + j, 1), :]
+                im = vt_ref[b, pl.ds(FDEV + g * JG + j, 1), :]
+                u.append(w[:RANK] * re + w[RANK:] * im)
+            return dot(jnp.concatenate(u, 0).astype(bf16), ohmt_ref[b])
+
+        def project_of(b, rows):
+            at = dot(rows, ohm_ref[b])
+            z = []
+            for c in range(2):
                 for j in range(JG):
-                    re = vt_ref[b, pl.ds(g * JG + j, 1), :]
-                    im = vt_ref[b, pl.ds(FDEV + g * JG + j, 1), :]
-                    u.append(w[:RANK] * re + w[RANK:] * im)
-                part = dot(jnp.concatenate(u, 0).astype(bf16), ohmt_ref[b])
-                return part if total is None else total + part
-
-            k = group_of[t]
-            first = None if chunks == 1 else jnp.zeros((RANK * JG, ROWS), f32)
-            sketch[k] = over(chunks, gather, first if sketch[k] is None else sketch[k])
+                    v = vt_ref[b, pl.ds(c * FDEV + g * JG + j, 1), :]
+                    z.append(at[j * RANK : (j + 1) * RANK] * v)
+            return dot(jnp.concatenate(z, 0).astype(bf16), ohht_ref[b])
+
+        sketch = [sketch_of(first[k]) for k in range(3)]
+        if not short:
+            for k in range(3):
+                sketch[k] = lax.fori_loop(
+                    1, filled[k], lambda q, x, k=k: x + sketch_of(first[k] + q), sketch[k]
+                )
         left, own, right = sketch
         sk = [x.astype(bf16) for x in sketch]
-        proj = None if chunks == 1 else jnp.zeros((2 * RANK * JG, 3 * HC), f32)
-        for t in range(SPAN):
-
-            def scatter(chunk, total, t=t):
-                b = t * chunks + chunk
-                at = dot(sk[group_of[t]], ohm_ref[b])
-                z = []
-                for c in range(2):
-                    for j in range(JG):
-                        v = vt_ref[b, pl.ds(c * FDEV + g * JG + j, 1), :]
-                        z.append(at[j * RANK : (j + 1) * RANK] * v)
-                part = dot(jnp.concatenate(z, 0).astype(bf16), ohht_ref[b])
-                return part if total is None else total + part
-
-            proj = over(chunks, scatter, proj)
+        proj = sum(project_of(first[k], sk[k]) for k in range(3))
+        if not short:
+            for k in range(3):
+                proj = lax.fori_loop(
+                    1, filled[k], lambda q, x, k=k: x + project_of(first[k] + q, sk[k]), proj
+                )
         full_left = jnp.where(lane < ROWS - RIM, left, pltpu.roll(own, ROWS - RIM, 1))
         full_right = jnp.where(lane < ROWS - RIM, right, pltpu.roll(own, ROWS - OWN_ROWS, 1))
         full_own = jnp.where(
@@ -266,15 +312,23 @@
                     at = (q2 * 4 + q) * RP
                     piece = gram[at : at + RANK, q2 * 4 * RP : (q2 + 1) * 4 * RP]
                     acc = jnp.where(lanes == q, piece, acc)
-                gram_ref[p, 2 * g + q2] = acc
+                gram_ref[p * (FDEV // 4) + 2 * g + q2] = acc
         return carry
 
-    lax.fori_loop(0, FDEV // JG, step, 0)
+    one_block = jnp.maximum(jnp.maximum(filled[0], filled[1]), filled[2]) <= 1
+
+    @pl.when(one_block)
+    def _():
+        lax.fori_loop(0, FDEV // JG, functools.partial(step, short=True), 0)
+
+    @pl.when(jnp.logical_not(one_block))
+    def _():
+        lax.fori_loop(0, FDEV // JG, functools.partial(step, short=False), 0)
 
 
 def invert_grams(gram_ref):
-    count = FDEV // 4
-    batch = 8
+    count = 3 * FDEV // 4
+    batch = 48
     wide = 4 * RP
     lane3 = iota((batch, RANK, wide), 2) % RP
     row3 = iota((batch, RANK, wide), 1)
@@ -283,25 +337,29 @@
     same = (iota((wide, wide), 0) // RP == iota((wide, wide), 1) // RP).astype(f32)
 
     def invert(i, carry):
-        p, c = i // (count // batch), i % (count // batch)
-        a = gram_ref[p, pl.ds(c * batch, batch)]
+        a = gram_ref[pl.ds(i * batch, batch)]
         diag = jnp.sum(jnp.where(lane3 == row3, a, 0.0), 1)
         trace = jnp.dot(
             diag, same, preferred_element_type=f32, precision=lax.Precision.HIGHEST
         )
         ridge = 0.01 * trace / RANK + 1e-06
         a = a + jnp.where(lane3 == row3, ridge[:, None, :], 0.0)
-        for k in range(RANK):
+        for k in range(0, RANK, 2):
             flat = a.reshape(batch * RANK, wide)
-            column = jnp.take_along_axis(flat, base + k, axis=1).reshape(batch, RANK, wide)
-            scale = 1.0 / column[:, k : k + 1]
-            pivot = jnp.where(lane1 == k, scale, a[:, k : k + 1] * scale)
-            rest = jnp.where(lane3 == k, 0.0, a) - column * pivot
-            a = jnp.where(row3 == k, pivot, rest)
-        gram_ref[p, pl.ds(c * batch, batch)] = a
+            c0 = jnp.take_along_axis(flat, base + k, axis=1).reshape(batch, RANK, wide)
+            c1 = jnp.take_along_axis(flat, base + k + 1, axis=1).reshape(batch, RANK, wide)
+            x, y, z = c0[:, k : k + 1], c1[:, k : k + 1], c1[:, k + 1 : k + 2]
+            scale = 1.0 / (x * z - y * y)
+            x, y, z = z * scale, -y * scale, x * scale
+            r0, r1 = a[:, k : k + 1], a[:, k + 1 : k + 2]
+            n0 = jnp.where(lane1 == k, x, jnp.where(lane1 == k + 1, y, x * r0 + y * r1))
+            n1 = jnp.where(lane1 == k, y, jnp.where(lane1 == k + 1, z, y * r0 + z * r1))
+            a = jnp.where(lane3 // 2 == k // 2, 0.0, a) - c0 * n0 - c1 * n1
+            a = jnp.where(row3 == k, n0, jnp.where(row3 == k + 1, n1, a))
+        gram_ref[pl.ds(i * batch, batch)] = a
         return carry
 
-    lax.fori_loop(0, 3 * count // batch, invert, 0)
+    lax.fori_loop(0, count // batch, invert, 0)
 
 
 def write(tiles, own_ref, pp_ref, gram_ref, out_ref, sem, freq_ref, cells_ref):
@@ -320,7 +378,7 @@
         rows = own_ref[i // 2, :, pl.ds(pl.multiple_of(i % 2 * wide, wide), wide)]
         weights = []
         for p in range(3):
-            inverse = gram_ref[p, i]
+            inverse = gram_ref[p * count + i]
             lanes = iota((RANK, wide), 1) // RP
             zero = jnp.zeros((RP - RANK, wide), f32)
             diag = []
@@ -374,6 +432,24 @@
         copy.wait()
 
 
+def patches(arrived, probe, tiles, slots):
+    return pl.pallas_call(
+        functools.partial(patch_kernel, tiles, slots),
+        out_shape=jax.ShapeDtypeStruct((OWN_ROWS, HC, COLS), f32),
+        in_specs=[pl.BlockSpec(memory_space=pltpu.VMEM)] * 2,
+        out_specs=pl.BlockSpec(memory_space=pl.ANY),
+        scratch_shapes=[
+            pltpu.VMEM((3, JG, RP, ROWS), f32),
+            pltpu.VMEM((3, FDEV, RP, COLS), f32),
+            pltpu.VMEM((FDEV // JG, OWN_ROWS, JG * RP), bf16),
+            pltpu.VMEM((3 * FDEV // 4, RANK, 4 * RP), f32),
+            pltpu.SemaphoreType.DMA((6,)),
+        ],
+        compiler_params=pltpu.CompilerParams(vmem_limit_bytes=60 * 2**20),
+        name="patches",
+    )(arrived, probe)
+
+
 def per_device(traces, bins, live, probe):
     tiles = lax.axis_size("grid")
     bands = lax.axis_size("freq")
@@ -404,21 +480,9 @@
         sent.reshape(sources, used + 2, COLS), ("grid", "freq"), 0, 0, tiled=True
     )
 
-    out = pl.pallas_call(
-        functools.partial(patch_kernel, tiles, slots),
-        out_shape=jax.ShapeDtypeStruct((OWN_ROWS, HC, COLS), f32),
-        in_specs=[vmem, vmem],
-        out_specs=pl.BlockSpec(memory_space=pl.ANY),
-        scratch_shapes=[
-            pltpu.VMEM((3, JG, RP, ROWS), f32),
-            pltpu.VMEM((3, FDEV, RP, COLS), f32),
-            pltpu.VMEM((FDEV // JG, OWN_ROWS, JG * RP), bf16),
-            pltpu.VMEM((3, FDEV // 4, RANK, 4 * RP), f32),
-            pltpu.SemaphoreType.DMA((6,)),
-        ],
-        compiler_params=pltpu.CompilerParams(vmem_limit_bytes=60 * 2**20),
-        name="patches",
-    )(arrived, jnp.transpose(probe, (1, 2, 0)).reshape(2 * RANK, HC))
+    out = patches(
+        arrived, jnp.transpose(probe, (1, 2, 0)).reshape(2 * RANK, HC), tiles, slots
+    )
     return out.reshape(OWNX, MY, HC, COLS)
 
 

time: 80.8 us -> 68.3 us (0.85)
  Pallas kernels: 51.4 us -> 38.8 us
    pallas_call x1, Pallas kernels: 50.2 us -> 37.6 us  [patches(): pl.pallas_call(functools.partial(patch_kernel, tiles, slots), out_shape=j...]
where the time goes in v1:
time: 68.3 us; the launch traced here: 68.1 us
  Pallas kernels  38.8 us (57%)
  blocking collectives  26.4 us (39%)
  other arithmetic  1.44 us (2%)
  local copies, waits for them, and re-layouts  1.18 us (2%)
    pallas_call x1, Pallas kernels, patches(): pl.pallas_call(functools.partial(patch_kernel, tiles, slots), out_shape=j...  37.6 us
    all_to_all x1, blocking collectives, per_device(): lax.all_to_all(sent.reshape(sources, used + 2, COLS), ('grid', 'freq'), 0...  26.4 us

profile of v1, /device:TPU:0, one launch (start us, length us, event | category | flops | bytes accessed | tf_op | source)
XLA Modules:
  0.0 68.1 jit_solution(15103152500347243280)
XLA Ops:
  0.0 0.7 %compare_bitcast_fusion = pred[8,1,16]{2,0,1:T(8,128)(4,1)S(1)} fusion(s32[1,8,16]{2,1,0:T(8,128)} %param.6), kind=kLoop, calls=%fused_computation.10 | loop fusion | flops 128 | bytes 640 | tf_op jit(solution)/shard_map/eq | solution.py:460
  0.7 0.7 %fusion = (bf16[8,1,16]{2,1,0:T(2,128)(2,1)S(1)}, s32[8,1,16]{2,1,0:T(1,128)S(1)}) fusion(pred[8,1,16]{2,0,1:T(8,128)(4,1)S(1)} %compare_bitcast_fusion, s32[8,1,16]{2,1,0:T(1,128)} %bitcast.14), kind=kLoop, calls=%fused_computation.7 | loop fusion | flops 2176 | bytes 1408 | tf_op jit(solution)/shard_map/convert
  1.5 0.1 concatenate.3
  1.6 0.0 copy-start
  1.6 1.0 %copy-done = bf16[1,8,16,2048]{3,2,1,0:T(8,128)(2,1)S(1)} copy-done((bf16[1,8,16,2048]{3,2,1,0:T(8,128)(2,1)S(1)}, bf16[1,8,16,2048]{3,2,1,0:T(8,128)(2,1)}, u32[]{:S(2)}) %copy-start) | copy-done | bytes 524312
  2.7 1.2 %spectra.1 = bf16[8,4,82,128]{3,2,1,0:T(8,128)(2,1)S(1)} custom-call(bf16[128,2048]{1,0:T(8,128)(2,1)S(1)} %bitcast.12, bf16[8,2,128]{2,1,0:T(2,128)(2,1)S(1)} %pad.9.marks_ref), custom_call_target="tpu_custom_call" | custom-call | tf_op jit(solution)/shard_map/spectra/pallas_call | solution.py:469
  3.9 26.4 %all_to_all.5.arrived_ref = bf16[32,82,128]{2,1,0:T(8,128)(2,1)} all-to-all(bf16[32,82,128]{2,1,0:T(8,128)(2,1)S(1)} %bitcast.11), channel_id=1, replica_groups=mesh['grid'=8,'freq'=4] {'grid','freq'}, dimensions={0} | all-to-all | bytes 1343488 | tf_op jit(solution)/shard_map/all_to_all | solution.py:479
  30.3 37.6 %patches.1 = f32[192,64,128]{2,1,0:T(8,128)} custom-call(bf16[32,82,128]{2,1,0:T(8,128)(2,1)} %all_to_all.5.arrived_ref, f32[48,64]{1,0:T(8,128)} %bitcast.13), custom_call_target="tpu_custom_call" | custom-call | tf_op jit(solution)/shard_map/patches/pallas_call | solution.py:436
  (4 shorter events, 0.1 us)
Async XLA Ops:
  1.6 1.0 %copy-start = (bf16[1,8,16,2048]{3,2,1,0:T(8,128)(2,1)S(1)}, bf16[1,8,16,2048]{3,2,1,0:T(8,128)(2,1)}, u32[]{:S(2)}) copy-start(bf16[1,8,16,2048]{3,2,1,0:T(8,128)(2,1)} %param.4) | copy-start | bytes 1572868

commit v2 on v1

--- a/solution.py
+++ b/solution.py
@@ -20,6 +20,7 @@
 OWN_ROWS = OWNX * MY
 RIM = MARGIN * MY
 ROWS = PX * MY
+PAIRS = OWN_ROWS // 2
 COLS = 2 * FDEV
 JG = 8
 RP = 32
@@ -52,10 +53,43 @@
     return jnp.cos(angle), jnp.sin(angle)
 
 
-def spectra_kernel(traces_ref, marks_ref, out_ref, table_ref):
+def marks_of(bins_ref, live_ref):
+    tiles, slots = bins_ref.shape
+    on = live_ref[...] == 1
+    both = jnp.concatenate(
+        [
+            jnp.where(on, bins_ref[...] // HC, int(DEAD)),
+            jnp.where(on, bins_ref[...] % HC, 0),
+        ],
+        0,
+    )
+    lanes = iota((slots, SPAN * COLS), 1)
+    put = (lanes % COLS == lanes // COLS * slots + iota((slots, SPAN * COLS), 0)).astype(f32)
+    placed = dot(both.astype(f32).astype(bf16), put.astype(bf16))
+    tile, lane = iota((tiles, COLS), 0), iota((tiles, COLS), 1)
+    marks = []
+    for i, other in enumerate((DEAD, 0.0)):
+        mark = jnp.full((tiles, COLS), other, f32)
+        for t in range(SPAN):
+            moved = placed[i * tiles : (i + 1) * tiles, t * COLS : (t + 1) * COLS]
+            if t != 2:
+                moved = pltpu.roll(moved, (2 - t) % tiles, 0)
+            there = (tile + (t - 2) >= 0) & (tile + (t - 2) < tiles) & (lane // slots == t)
+            mark = jnp.where(there, moved, mark)
+        marks.append(mark.astype(bf16))
+    return marks
+
+
+def spectra_kernel(
+    traces_ref, bins_ref, live_ref, out_ref, table_ref, held_ref, bins_held, live_held, sem
+):
     length, width = table_ref.shape
     tiles, bands = out_ref.shape[:2]
-    slots = traces_ref.shape[0] // tiles
+    slots = bins_ref.shape[1]
+    moves = ((bins_ref, bins_held), (live_ref, live_held), (traces_ref, held_ref))
+    copies = [pltpu.make_async_copy(a, b, sem.at[i]) for i, (a, b) in enumerate(moves)]
+    for copy in copies:
+        copy.start()
     coarse = length // 64
     column = iota((1, width), 1)
     col = lambda n: column + jnp.zeros((n, 1), jnp.int32)
@@ -69,7 +103,10 @@
     for i in range(coarse):
         block = c1[i : i + 1] * fine_c - s1[i : i + 1] * fine_s
         table_ref[64 * i : 64 * i + 64, :] = block.astype(bf16)
-    spectra = dot(traces_ref[...], table_ref[...]).astype(bf16)
+    for copy in copies:
+        copy.wait()
+    marks = marks_of(bins_held, live_held)
+    spectra = dot(held_ref[...], table_ref[...]).astype(bf16)
     nothing = jnp.zeros((slots, COLS), bf16)
     for band in range(bands):
         piece = spectra[:, band * COLS : (band + 1) * COLS]
@@ -80,7 +117,9 @@
                 out_ref[tile, band, t * slots : (t + 1) * slots, :] = (
                     piece[source * slots : (source + 1) * slots] if there else nothing
                 )
-            out_ref[tile, band, SPAN * slots : SPAN * slots + 2, :] = marks_ref[tile]
+            out_ref[tile, band, SPAN * slots : SPAN * slots + 2, :] = jnp.concatenate(
+                [x[tile : tile + 1] for x in marks], 0
+            )
 
 
 def patch_kernel(
@@ -114,7 +153,7 @@
     invert_grams(gram_ref)
     pl.run_scoped(
         functools.partial(write, tiles, own_ref, pp_ref, gram_ref, out_ref, sem),
-        pltpu.VMEM((FDEV, OWN_ROWS, COLS), f32),
+        pltpu.VMEM((PAIRS, COLS, 2 * HC), f32),
         pltpu.VMEM((OWN_ROWS, HC, COLS), f32),
     )
 
@@ -236,6 +275,8 @@
     for k in range(3):
         pack(k, jnp.int32(0))
 
+    for k in range(3):
+
         def more(q, carry, k=k):
             pack(k, q)
             return carry
@@ -303,7 +344,9 @@
             pp_ref[p, pl.ds(g * JG, JG), :RANK, :] = parts[p].reshape(JG, RANK, COLS)
             pad = st_ref[p].reshape(JG * RP, ROWS).astype(bf16)
             if p == 1:
-                own_ref[g] = st_ref[p].reshape(JG * RP, ROWS).T[:OWN_ROWS].astype(bf16)
+                for q2 in range(2):
+                    quad = st_ref[p, 4 * q2 : 4 * q2 + 4].reshape(4 * RP, ROWS)
+                    own_ref[2 * g + q2] = quad.T
             gram = lax.dot_general(pad, pad, (((1,), (1,)), ((), ())), preferred_element_type=f32)
             for q2 in range(2):
                 lanes = iota((RANK, 4 * RP), 1) // RP
@@ -319,7 +362,7 @@
 
     @pl.when(one_block)
     def _():
-        lax.fori_loop(0, FDEV // JG, functools.partial(step, short=True), 0)
+        lax.fori_loop(0, FDEV // JG, functools.partial(step, short=True), 0, unroll=4)
 
     @pl.when(jnp.logical_not(one_block))
     def _():
@@ -368,53 +411,63 @@
     here = lax.axis_index("grid")
     has_left = (here > 0).astype(f32)
     has_right = (here < tiles - 1).astype(f32)
-    edge = iota((RIM, 1), 0) < MY
+    rim = RIM // 2
+    edge = iota((rim * JG, 1), 0) < MY // 2 * JG
     taper_first = jnp.where(edge, 0.6, 0.8)
     taper_last = jnp.where(edge, 0.8, 0.6)
     left_w = jnp.where(edge, 0.4, 0.2) * has_left
     right_w = jnp.where(edge, 0.2, 0.4) * has_right
-
-    def rebuild(i, carry):
-        rows = own_ref[i // 2, :, pl.ds(pl.multiple_of(i % 2 * wide, wide), wide)]
-        weights = []
+    lo = iota((wide, COLS), 1) < HC
+    mine = [iota((JG, wide), 1) // RP + 4 * q2 == iota((JG, wide), 0) for q2 in range(2)]
+
+    def rebuild(g, carry):
+        rows = []
+        for m in range(PAIRS):
+            row = []
+            for parity in range(2):
+                for q2 in range(2):
+                    x = own_ref[2 * g + q2, pl.ds(2 * m + parity, 1), :]
+                    row.append(jnp.where(mine[q2], x, 0.0))
+            rows.append(jnp.concatenate(row, 1))
+        rows = jnp.concatenate(rows, 0).astype(bf16)
+        w = []
         for p in range(3):
-            inverse = gram_ref[p * count + i]
-            lanes = iota((RANK, wide), 1) // RP
-            zero = jnp.zeros((RP - RANK, wide), f32)
-            diag = []
-            for q in range(4):
-                diag += [jnp.where(lanes == q, inverse, 0.0), zero]
-            b_high, b_low = split(jnp.concatenate(diag, 0))
-            p_high, p_low = split(pp_ref[p, pl.ds(i * 4, 4)].reshape(wide, COLS))
-            coeff = dot(b_high, p_high) + dot(b_high, p_low) + dot(b_low, p_high)
-            weights.append(coeff)
-        quarter = iota((wide, COLS), 0) // RP
-        for a in range(2):
-            w = [
-                jnp.concatenate([jnp.where(quarter == 2 * a + e, x, 0.0) for e in range(2)], 1).astype(bf16)
-                for x in weights
-            ]
-            mid = dot(rows, w[1])
-            first = mid[:RIM] * taper_first + dot(rows[:RIM], w[0]) * left_w
-            last = mid[OWN_ROWS - RIM :] * taper_last + dot(rows[OWN_ROWS - RIM :], w[2]) * right_w
-            full = jnp.concatenate([first, mid[RIM : OWN_ROWS - RIM], last], 0)
-            for e in range(2):
-                freq_ref[i * 4 + 2 * a + e] = full[:, e * COLS : (e + 1) * COLS]
+            even, odd = [], []
+            for q2 in range(2):
+                i = 2 * g + q2
+                inverse = gram_ref[p * count + i]
+                lanes = iota((RANK, wide), 1) // RP
+                zero = jnp.zeros((RP - RANK, wide), f32)
+                diag = []
+                for q in range(4):
+                    diag += [jnp.where(lanes == q, inverse, 0.0), zero]
+                b_high, b_low = split(jnp.concatenate(diag, 0))
+                p_high, p_low = split(pp_ref[p, pl.ds(i * 4, 4)].reshape(wide, COLS))
+                twice = dot(b_high, jnp.concatenate([p_high, p_low], 1))
+                c = twice[:, :COLS] + twice[:, COLS:] + dot(b_low, p_high)
+                r = pltpu.roll(c, HC, 1)
+                even.append(jnp.concatenate([jnp.where(lo, c, 0.0), jnp.where(lo, r, 0.0)], 1))
+                odd.append(jnp.concatenate([jnp.where(lo, 0.0, r), jnp.where(lo, 0.0, c)], 1))
+            w.append(jnp.concatenate(even + odd, 0).astype(bf16))
+        mid = dot(rows, w[1])
+        first, last = rim * JG, (PAIRS - rim) * JG
+        begin = mid[:first] * taper_first + dot(rows[:first], w[0]) * left_w
+        end = mid[last:] * taper_last + dot(rows[last:], w[2]) * right_w
+        full = jnp.concatenate([begin, mid[first:last], end], 0)
+        for c in range(2):
+            part = full[:, c * COLS : (c + 1) * COLS].reshape(PAIRS, JG, COLS)
+            freq_ref[:, pl.ds(pl.multiple_of(c * FDEV + g * JG, JG), JG), :] = part
         return carry
 
-    lax.fori_loop(0, count, rebuild, 0)
-
-    unroll = 4
-    half_lane = iota((HC, COLS), 1) < FDEV
+    lax.fori_loop(0, FDEV // JG, rebuild, 0, unroll=2)
+
+    unroll = 8
 
     def turn(i, carry):
         for q in range(unroll):
-            m = (i * unroll + q) * 2
-            both = jnp.concatenate([freq_ref[:, m, :], freq_ref[:, m + 1, :]], 0)
-            flip = both.T
-            re, im = flip[:HC], flip[HC:]
-            cells_ref[m] = jnp.where(half_lane, re, pltpu.roll(im, FDEV, 1))
-            cells_ref[m + 1] = jnp.where(half_lane, pltpu.roll(re, FDEV, 1), im)
+            m = i * unroll + q
+            flip = freq_ref[m].T
+            cells_ref[pl.ds(2 * m, 2)] = flip.reshape(2, HC, COLS)
         return carry
 
     pieces = 6
@@ -441,7 +494,7 @@
         scratch_shapes=[
             pltpu.VMEM((3, JG, RP, ROWS), f32),
             pltpu.VMEM((3, FDEV, RP, COLS), f32),
-            pltpu.VMEM((FDEV // JG, OWN_ROWS, JG * RP), bf16),
+            pltpu.VMEM((FDEV // 4, ROWS, 4 * RP), f32),
             pltpu.VMEM((3 * FDEV // 4, RANK, 4 * RP), f32),
             pltpu.SemaphoreType.DMA((6,)),
         ],
@@ -457,24 +510,22 @@
     sources = tiles * bands
     used = SPAN * slots
 
-    on = live[0] == 1
-    mark = jnp.stack(
-        [jnp.where(on, bins[0] // HC, int(DEAD)), jnp.where(on, bins[0] % HC, 0)], 1
-    ).astype(bf16)
-    mark = jnp.pad(mark, ((2, 2), (0, 0), (0, 0)), constant_values=DEAD)
-    marks = jnp.concatenate([mark[t : t + tiles] for t in range(SPAN)], 2)
-    marks = jnp.pad(marks, ((0, 0), (0, 0), (0, COLS - used)))
-
     vmem = pl.BlockSpec(memory_space=pltpu.VMEM)
     sent = pl.pallas_call(
         spectra_kernel,
         out_shape=jax.ShapeDtypeStruct((tiles, bands, used + 2, COLS), bf16),
-        in_specs=[vmem, vmem],
+        in_specs=[pl.BlockSpec(memory_space=pl.ANY)] * 3,
         out_specs=vmem,
-        scratch_shapes=[pltpu.VMEM((length, COLS * bands), bf16)],
-        compiler_params=pltpu.CompilerParams(vmem_limit_bytes=48 * 2**20),
+        scratch_shapes=[
+            pltpu.VMEM((length, COLS * bands), bf16),
+            pltpu.VMEM((tiles * slots, length), bf16),
+            pltpu.VMEM((tiles, slots), jnp.int32),
+            pltpu.VMEM((tiles, slots), jnp.int32),
+            pltpu.SemaphoreType.DMA((3,)),
+        ],
+        compiler_params=pltpu.CompilerParams(vmem_limit_bytes=60 * 2**20),
         name="spectra",
-    )(traces.reshape(tiles * slots, length), marks)
+    )(traces.reshape(tiles * slots, length), bins[0], live[0])
 
     arrived = lax.all_to_all(
         sent.reshape(sources, used + 2, COLS), ("grid", "freq"), 0, 0, tiled=True

time: 68.3 us -> 55.9 us (0.82)
  Pallas kernels: 38.8 us -> 28.9 us
  other arithmetic: 1.44 us -> 0 us
  local copies, waits for them, and re-layouts: 1.18 us -> 0 us
    pallas_call x1, Pallas kernels: 37.6 us -> 26.3 us  [patches(): pl.pallas_call(functools.partial(patch_kernel, tiles, slots), out_shape=j...]
    pallas_call x1, Pallas kernels: 1.18 us -> 2.54 us  [per_device(): pl.pallas_call(spectra_kernel, out_shape=jax.ShapeDtypeStruct((tiles, ban...]
    unnamed x2 -> x0, local copies, waits for them, and re-layouts: 1.04 us -> none
    another operation x3 -> x0, other arithmetic: 0.75 us -> none
    eq x1 -> x0, other arithmetic: 0.69 us -> none  [per_device(): on = live[0] == 1]
where the time goes in v2:
time: 55.9 us; the launch traced here: 55.7 us
  Pallas kernels  28.9 us (52%)
  blocking collectives  26.6 us (48%)
    all_to_all x1, blocking collectives, per_device(): lax.all_to_all(sent.reshape(sources, used + 2, COLS), ('grid', 'freq'), 0...  26.6 us
    pallas_call x1, Pallas kernels, patches(): pl.pallas_call(functools.partial(patch_kernel, tiles, slots), out_shape=j...  26.3 us
    pallas_call x1, Pallas kernels, per_device(): pl.pallas_call(spectra_kernel, out_shape=jax.ShapeDtypeStruct((tiles, ban...  2.54 us

profile of v2, /device:TPU:0, one launch (start us, length us, event | category | flops | bytes accessed | tf_op | source)
XLA Modules:
  0.0 55.7 jit_solution(12239163848838141262)
XLA Ops:
  0.0 2.5 %spectra.1 = bf16[8,4,82,128]{3,2,1,0:T(8,128)(2,1)} custom-call(bf16[128,2048]{1,0:T(8,128)(2,1)} %bitcast.9, s32[8,16]{1,0:T(8,128)} %bitcast.11, s32[8,16]{1,0:T(8,128)} %bitcast.12), custom_call_target="tpu_custom_call" | custom-call | tf_op jit(solution)/shard_map/spectra/pallas_call | solution.py:514
  2.6 26.6 %all_to_all.5.arrived_ref = bf16[32,82,128]{2,1,0:T(8,128)(2,1)} all-to-all(bf16[32,82,128]{2,1,0:T(8,128)(2,1)} %bitcast.8), channel_id=1, replica_groups=mesh['grid'=8,'freq'=4] {'grid','freq'}, dimensions={0} | all-to-all | bytes 1343488 | tf_op jit(solution)/shard_map/all_to_all | solution.py:530
  29.2 26.3 %patches.1 = f32[192,64,128]{2,1,0:T(8,128)} custom-call(bf16[32,82,128]{2,1,0:T(8,128)(2,1)} %all_to_all.5.arrived_ref, f32[48,64]{1,0:T(8,128)} %bitcast.10), custom_call_target="tpu_custom_call" | custom-call | tf_op jit(solution)/shard_map/patches/pallas_call | solution.py:489

commit v3 on v2

--- a/solution.py
+++ b/solution.py
@@ -26,6 +26,8 @@
 RP = 32
 BLOCK_SRC = 32
 DEAD = 255.0
+UNROLL = 4
+PER_STEP = 3
 
 f32 = jnp.float32
 bf16 = jnp.bfloat16
@@ -131,7 +133,8 @@
     st_ref,
     pp_ref,
     own_ref,
-    gram_ref,
+    first_ref,
+    second_ref,
     sem,
 ):
     sources = arrived_ref.shape[0]
@@ -141,7 +144,9 @@
     side = chunks + rim_blocks(chunks, n)
     nb = chunks + 2 * side
     pl.run_scoped(
-        functools.partial(project, slots, arrived_ref, probe_ref, st_ref, pp_ref, own_ref, gram_ref),
+        functools.partial(
+            project, slots, arrived_ref, probe_ref, st_ref, pp_ref, own_ref, first_ref, second_ref
+        ),
         pltpu.VMEM((nb, COLS, n), f32),
         pltpu.VMEM((nb, 2 * RANK, n), f32),
         pltpu.VMEM((nb, ROWS, n), bf16),
@@ -150,9 +155,8 @@
         pltpu.VMEM((SPAN * chunks, 1, n), f32),
         pltpu.VMEM((SPAN * chunks, 8, n), f32),
     )
-    invert_grams(gram_ref)
     pl.run_scoped(
-        functools.partial(write, tiles, own_ref, pp_ref, gram_ref, out_ref, sem),
+        functools.partial(write, tiles, own_ref, pp_ref, first_ref, second_ref, out_ref, sem),
         pltpu.VMEM((PAIRS, COLS, 2 * HC), f32),
         pltpu.VMEM((OWN_ROWS, HC, COLS), f32),
     )
@@ -175,7 +179,8 @@
     st_ref,
     pp_ref,
     own_ref,
-    gram_ref,
+    first_ref,
+    second_ref,
     vt_ref,
     wt_ref,
     ohm_ref,
@@ -287,7 +292,7 @@
     pp_ref[:, :, RANK:, :] = jnp.zeros((3, FDEV, RP - RANK, COLS), f32)
     lane = iota((RANK * JG, ROWS), 1)
 
-    def step(g, carry, short):
+    def step(g, carry, short, gram_ref, start):
         def sketch_of(b):
             w = wt_ref[b]
             u = []
@@ -355,57 +360,69 @@
                     at = (q2 * 4 + q) * RP
                     piece = gram[at : at + RANK, q2 * 4 * RP : (q2 + 1) * 4 * RP]
                     acc = jnp.where(lanes == q, piece, acc)
-                gram_ref[p * (FDEV // 4) + 2 * g + q2] = acc
+                gram_ref[:, p * (FDEV // 8) + 2 * (g - start) + q2, :] = acc
         return carry
 
     one_block = jnp.maximum(jnp.maximum(filled[0], filled[1]), filled[2]) <= 1
+
+    steps = FDEV // JG
+    half = steps // 2
 
     @pl.when(one_block)
     def _():
-        lax.fori_loop(0, FDEV // JG, functools.partial(step, short=True), 0, unroll=4)
+        early = functools.partial(step, short=True, gram_ref=first_ref, start=0)
+        lax.fori_loop(0, half, early, 0, unroll=UNROLL)
+        work = invert(first_ref)
+        for g in range(half, steps):
+            for _ in range(PER_STEP):
+                next(work, None)
+            step(g, 0, True, second_ref, half)
+        for _ in work:
+            pass
 
     @pl.when(jnp.logical_not(one_block))
     def _():
-        lax.fori_loop(0, FDEV // JG, functools.partial(step, short=False), 0)
-
-
-def invert_grams(gram_ref):
-    count = 3 * FDEV // 4
-    batch = 48
+        for i, ref in enumerate((first_ref, second_ref)):
+            body = functools.partial(step, short=False, gram_ref=ref, start=i * half)
+            lax.fori_loop(i * half, (i + 1) * half, body, 0)
+        for _ in invert(first_ref):
+            pass
+
+
+def invert(gram_ref):
     wide = 4 * RP
-    lane3 = iota((batch, RANK, wide), 2) % RP
-    row3 = iota((batch, RANK, wide), 1)
-    lane1 = iota((batch, 1, wide), 2) % RP
-    base = iota((batch * RANK, wide), 1) // RP * RP
+    count = gram_ref.shape[1]
+    lane = iota((count, wide), 1) % RP
+    base = iota((count, wide), 1) // RP * RP
     same = (iota((wide, wide), 0) // RP == iota((wide, wide), 1) // RP).astype(f32)
-
-    def invert(i, carry):
-        a = gram_ref[pl.ds(i * batch, batch)]
-        diag = jnp.sum(jnp.where(lane3 == row3, a, 0.0), 1)
-        trace = jnp.dot(
-            diag, same, preferred_element_type=f32, precision=lax.Precision.HIGHEST
-        )
-        ridge = 0.01 * trace / RANK + 1e-06
-        a = a + jnp.where(lane3 == row3, ridge[:, None, :], 0.0)
-        for k in range(0, RANK, 2):
-            flat = a.reshape(batch * RANK, wide)
-            c0 = jnp.take_along_axis(flat, base + k, axis=1).reshape(batch, RANK, wide)
-            c1 = jnp.take_along_axis(flat, base + k + 1, axis=1).reshape(batch, RANK, wide)
-            x, y, z = c0[:, k : k + 1], c1[:, k : k + 1], c1[:, k + 1 : k + 2]
-            scale = 1.0 / (x * z - y * y)
-            x, y, z = z * scale, -y * scale, x * scale
-            r0, r1 = a[:, k : k + 1], a[:, k + 1 : k + 2]
-            n0 = jnp.where(lane1 == k, x, jnp.where(lane1 == k + 1, y, x * r0 + y * r1))
-            n1 = jnp.where(lane1 == k, y, jnp.where(lane1 == k + 1, z, y * r0 + z * r1))
-            a = jnp.where(lane3 // 2 == k // 2, 0.0, a) - c0 * n0 - c1 * n1
-            a = jnp.where(row3 == k, n0, jnp.where(row3 == k + 1, n1, a))
-        gram_ref[pl.ds(i * batch, batch)] = a
-        return carry
-
-    lax.fori_loop(0, count // batch, invert, 0)
-
-
-def write(tiles, own_ref, pp_ref, gram_ref, out_ref, sem, freq_ref, cells_ref):
+    a = [gram_ref[r] for r in range(RANK)]
+    diag = jnp.zeros((count, wide), f32)
+    for r in range(RANK):
+        diag = jnp.where(lane == r, a[r], diag)
+    trace = jnp.dot(diag, same, preferred_element_type=f32, precision=lax.Precision.HIGHEST)
+    ridge = 0.01 * trace / RANK + 1e-06
+    a = [jnp.where(lane == r, a[r] + ridge, a[r]) for r in range(RANK)]
+    for k in range(0, RANK, 2):
+        c0 = [jnp.take_along_axis(x, base + k, axis=1) for x in a]
+        c1 = [jnp.take_along_axis(x, base + (k + 1), axis=1) for x in a]
+        x, y, z = c0[k], c1[k], c1[k + 1]
+        scale = 1.0 / (x * z - y * y)
+        x, y, z = z * scale, -y * scale, x * scale
+        n0 = jnp.where(lane == k, x, jnp.where(lane == k + 1, y, x * a[k] + y * a[k + 1]))
+        n1 = jnp.where(lane == k, y, jnp.where(lane == k + 1, z, y * a[k] + z * a[k + 1]))
+        pair = lane // 2 == k // 2
+        for r in range(RANK):
+            if r // 2 != k // 2:
+                a[r] = jnp.where(pair, 0.0, a[r]) - c0[r] * n0 - c1[r] * n1
+        a[k], a[k + 1] = n0, n1
+        yield
+    for r in range(RANK):
+        gram_ref[r] = a[r]
+
+
+def write(
+    tiles, own_ref, pp_ref, first_ref, second_ref, out_ref, sem, freq_ref, cells_ref
+):
     count = FDEV // 4
     wide = 4 * RP
     here = lax.axis_index("grid")
@@ -420,7 +437,7 @@
     lo = iota((wide, COLS), 1) < HC
     mine = [iota((JG, wide), 1) // RP + 4 * q2 == iota((JG, wide), 0) for q2 in range(2)]
 
-    def rebuild(g, carry):
+    def rebuild(g, carry, gram_ref, start):
         rows = []
         for m in range(PAIRS):
             row = []
@@ -435,7 +452,7 @@
             even, odd = [], []
             for q2 in range(2):
                 i = 2 * g + q2
-                inverse = gram_ref[p * count + i]
+                inverse = gram_ref[:, p * (FDEV // 8) + i - 2 * start, :]
                 lanes = iota((RANK, wide), 1) // RP
                 zero = jnp.zeros((RP - RANK, wide), f32)
                 diag = []
@@ -459,7 +476,17 @@
             freq_ref[:, pl.ds(pl.multiple_of(c * FDEV + g * JG, JG), JG), :] = part
         return carry
 
-    lax.fori_loop(0, FDEV // JG, rebuild, 0, unroll=2)
+    steps = FDEV // JG
+    half = steps // 2
+    work = invert(second_ref)
+    for g in range(half):
+        for _ in range(PER_STEP):
+            next(work, None)
+        rebuild(g, 0, first_ref, 0)
+    for _ in work:
+        pass
+    late = functools.partial(rebuild, gram_ref=second_ref, start=half)
+    lax.fori_loop(half, steps, late, 0, unroll=2)
 
     unroll = 8
 
@@ -495,7 +522,8 @@
             pltpu.VMEM((3, JG, RP, ROWS), f32),
             pltpu.VMEM((3, FDEV, RP, COLS), f32),
             pltpu.VMEM((FDEV // 4, ROWS, 4 * RP), f32),
-            pltpu.VMEM((3 * FDEV // 4, RANK, 4 * RP), f32),
+            pltpu.VMEM((RANK, 3 * FDEV // 8, 4 * RP), f32),
+            pltpu.VMEM((RANK, 3 * FDEV // 8, 4 * RP), f32),
             pltpu.SemaphoreType.DMA((6,)),
         ],
         compiler_params=pltpu.CompilerParams(vmem_limit_bytes=60 * 2**20),

time: 55.9 us -> 52.7 us (0.943)
  Pallas kernels: 28.9 us -> 25.7 us
    pallas_call x1, Pallas kernels: 26.3 us -> 23.1 us  [patches(): pl.pallas_call(functools.partial(patch_kernel, tiles, slots), out_shape=j...]
where the time goes in v3:
time: 52.7 us; the launch traced here: 52.5 us
  blocking collectives  26.6 us (50%)
  Pallas kernels  25.7 us (49%)
    all_to_all x1, blocking collectives, per_device(): lax.all_to_all(sent.reshape(sources, used + 2, COLS), ('grid', 'freq'), 0...  26.6 us
    pallas_call x1, Pallas kernels, patches(): pl.pallas_call(functools.partial(patch_kernel, tiles, slots), out_shape=j...  23.1 us
    pallas_call x1, Pallas kernels, per_device(): pl.pallas_call(spectra_kernel, out_shape=jax.ShapeDtypeStruct((tiles, ban...  2.54 us

profile of v3, /device:TPU:0, one launch (start us, length us, event | category | flops | bytes accessed | tf_op | source)
XLA Modules:
  0.0 52.5 jit_solution(17149646904092120166)
XLA Ops:
  0.0 2.5 %spectra.1 = bf16[8,4,82,128]{3,2,1,0:T(8,128)(2,1)} custom-call(bf16[128,2048]{1,0:T(8,128)(2,1)} %bitcast.9, s32[8,16]{1,0:T(8,128)} %bitcast.11, s32[8,16]{1,0:T(8,128)} %bitcast.12), custom_call_target="tpu_custom_call" | custom-call | tf_op jit(solution)/shard_map/spectra/pallas_call | solution.py:542
  2.6 26.6 %all_to_all.5.arrived_ref = bf16[32,82,128]{2,1,0:T(8,128)(2,1)} all-to-all(bf16[32,82,128]{2,1,0:T(8,128)(2,1)} %bitcast.8), channel_id=1, replica_groups=mesh['grid'=8,'freq'=4] {'grid','freq'}, dimensions={0} | all-to-all | bytes 1343488 | tf_op jit(solution)/shard_map/all_to_all | solution.py:558
  29.2 23.1 %patches.1 = f32[192,64,128]{2,1,0:T(8,128)} custom-call(bf16[32,82,128]{2,1,0:T(8,128)(2,1)} %all_to_all.5.arrived_ref, f32[48,64]{1,0:T(8,128)} %bitcast.10), custom_call_target="tpu_custom_call" | custom-call | tf_op jit(solution)/shard_map/patches/pallas_call | solution.py:516

commit v4 on v3

--- a/solution.py
+++ b/solution.py
@@ -159,6 +159,8 @@
         functools.partial(write, tiles, own_ref, pp_ref, first_ref, second_ref, out_ref, sem),
         pltpu.VMEM((PAIRS, COLS, 2 * HC), f32),
         pltpu.VMEM((OWN_ROWS, HC, COLS), f32),
+        pltpu.VMEM((FDEV // JG // 2, 3, 2 * JG * RP, 2 * COLS), bf16),
+        pltpu.VMEM((FDEV // JG, 2, 2, RIM, 4 * RP), f32),
     )
 
 
@@ -352,12 +354,14 @@
                 for q2 in range(2):
                     quad = st_ref[p, 4 * q2 : 4 * q2 + 4].reshape(4 * RP, ROWS)
                     own_ref[2 * g + q2] = quad.T
-            gram = lax.dot_general(pad, pad, (((1,), (1,)), ((), ())), preferred_element_type=f32)
+            gram = lax.dot_general(
+                whole.astype(bf16), pad, (((1,), (1,)), ((), ())), preferred_element_type=f32
+            )
             for q2 in range(2):
                 lanes = iota((RANK, 4 * RP), 1) // RP
                 acc = jnp.zeros((RANK, 4 * RP), f32)
                 for q in range(4):
-                    at = (q2 * 4 + q) * RP
+                    at = (q2 * 4 + q) * RANK
                     piece = gram[at : at + RANK, q2 * 4 * RP : (q2 + 1) * 4 * RP]
                     acc = jnp.where(lanes == q, piece, acc)
                 gram_ref[:, p * (FDEV // 8) + 2 * (g - start) + q2, :] = acc
@@ -421,7 +425,17 @@
 
 
 def write(
-    tiles, own_ref, pp_ref, first_ref, second_ref, out_ref, sem, freq_ref, cells_ref
+    tiles,
+    own_ref,
+    pp_ref,
+    first_ref,
+    second_ref,
+    out_ref,
+    sem,
+    freq_ref,
+    cells_ref,
+    weights_ref,
+    rim_ref,
 ):
     count = FDEV // 4
     wide = 4 * RP
@@ -437,16 +451,23 @@
     lo = iota((wide, COLS), 1) < HC
     mine = [iota((JG, wide), 1) // RP + 4 * q2 == iota((JG, wide), 0) for q2 in range(2)]
 
-    def rebuild(g, carry, gram_ref, start):
+    def expand(take, pairs):
         rows = []
-        for m in range(PAIRS):
+        for m in pairs:
             row = []
             for parity in range(2):
                 for q2 in range(2):
-                    x = own_ref[2 * g + q2, pl.ds(2 * m + parity, 1), :]
-                    row.append(jnp.where(mine[q2], x, 0.0))
+                    row.append(jnp.where(mine[q2], take(q2, 2 * m + parity), 0.0))
             rows.append(jnp.concatenate(row, 1))
-        rows = jnp.concatenate(rows, 0).astype(bf16)
+        return jnp.concatenate(rows, 0).astype(bf16)
+
+    def own_rows(g, pairs):
+        return expand(lambda q2, m: own_ref[2 * g + q2, pl.ds(m, 1), :], pairs)
+
+    def rim_rows(g, side):
+        return expand(lambda q2, m: rim_ref[g, side, q2, pl.ds(m, 1), :], range(rim))
+
+    def weights(g, gram_ref, start):
         w = []
         for p in range(3):
             even, odd = [], []
@@ -459,53 +480,64 @@
                 for q in range(4):
                     diag += [jnp.where(lanes == q, inverse, 0.0), zero]
                 b_high, b_low = split(jnp.concatenate(diag, 0))
-                p_high, p_low = split(pp_ref[p, pl.ds(i * 4, 4)].reshape(wide, COLS))
-                twice = dot(b_high, jnp.concatenate([p_high, p_low], 1))
-                c = twice[:, :COLS] + twice[:, COLS:] + dot(b_low, p_high)
+                c = pp_ref[p, pl.ds(i * 4, 4)].reshape(wide, COLS)
+                if p == 1:
+                    p_high, p_low = split(c)
+                    twice = dot(b_high, jnp.concatenate([p_high, p_low], 1))
+                    c = twice[:, :COLS] + twice[:, COLS:] + dot(b_low, p_high)
+                else:
+                    edge_rows = pl.ds(0 if p == 0 else OWN_ROWS - RIM, RIM)
+                    x = own_ref[i, edge_rows, :].astype(bf16)
+                    twice = dot(x, jnp.concatenate([b_high, b_low], 1))
+                    rim_ref[g, p // 2, q2] = twice[:, :wide] + twice[:, wide:]
                 r = pltpu.roll(c, HC, 1)
                 even.append(jnp.concatenate([jnp.where(lo, c, 0.0), jnp.where(lo, r, 0.0)], 1))
                 odd.append(jnp.concatenate([jnp.where(lo, 0.0, r), jnp.where(lo, 0.0, c)], 1))
             w.append(jnp.concatenate(even + odd, 0).astype(bf16))
-        mid = dot(rows, w[1])
-        first, last = rim * JG, (PAIRS - rim) * JG
-        begin = mid[:first] * taper_first + dot(rows[:first], w[0]) * left_w
-        end = mid[last:] * taper_last + dot(rows[last:], w[2]) * right_w
-        full = jnp.concatenate([begin, mid[first:last], end], 0)
+        return w
+
+    def put(pairs, g, full):
         for c in range(2):
-            part = full[:, c * COLS : (c + 1) * COLS].reshape(PAIRS, JG, COLS)
-            freq_ref[:, pl.ds(pl.multiple_of(c * FDEV + g * JG, JG), JG), :] = part
-        return carry
+            part = full[:, c * COLS : (c + 1) * COLS].reshape(len(pairs), JG, COLS)
+            at = pl.ds(c * FDEV + g * JG, JG)
+            freq_ref[pairs.start : pairs.stop, at, :] = part
 
     steps = FDEV // JG
     half = steps // 2
     work = invert(second_ref)
+    blocks = PAIRS // rim
     for g in range(half):
         for _ in range(PER_STEP):
             next(work, None)
-        rebuild(g, 0, first_ref, 0)
+        w = weights(g, first_ref, 0)
+        mid = dot(own_rows(g, range(PAIRS)), w[1])
+        first, last = rim * JG, (PAIRS - rim) * JG
+        begin = mid[:first] * taper_first + dot(rim_rows(g, 0), w[0]) * left_w
+        end = mid[last:] * taper_last + dot(rim_rows(g, 1), w[2]) * right_w
+        put(range(PAIRS), g, jnp.concatenate([begin, mid[first:last], end], 0))
     for _ in work:
         pass
-    late = functools.partial(rebuild, gram_ref=second_ref, start=half)
-    lax.fori_loop(half, steps, late, 0, unroll=2)
-
-    unroll = 8
-
-    def turn(i, carry):
-        for q in range(unroll):
-            m = i * unroll + q
-            flip = freq_ref[m].T
-            cells_ref[pl.ds(2 * m, 2)] = flip.reshape(2, HC, COLS)
+
+    def late(g, carry):
+        for p, x in enumerate(weights(g, second_ref, half)):
+            weights_ref[g - half, p] = x
         return carry
 
-    pieces = 6
-    size = OWN_ROWS // pieces
+    lax.fori_loop(half, steps, late, 0, unroll=4)
     copies = []
-    for k in range(pieces):
-        per_piece = size // (2 * unroll)
-        lax.fori_loop(k * per_piece, (k + 1) * per_piece, turn, 0)
-        copy = pltpu.make_async_copy(
-            cells_ref.at[pl.ds(k * size, size)], out_ref.at[pl.ds(k * size, size)], sem.at[k]
-        )
+    for b in range(blocks):
+        pairs = range(b * rim, (b + 1) * rim)
+        for g in range(half, steps):
+            part = dot(own_rows(g, pairs), weights_ref[g - half, 1])
+            if b == 0:
+                part = part * taper_first + dot(rim_rows(g, 0), weights_ref[g - half, 0]) * left_w
+            elif b == blocks - 1:
+                part = part * taper_last + dot(rim_rows(g, 1), weights_ref[g - half, 2]) * right_w
+            put(pairs, g, part)
+        for m in pairs:
+            cells_ref[2 * m : 2 * m + 2] = freq_ref[m].T.reshape(2, HC, COLS)
+        cells = pl.ds(2 * rim * b, 2 * rim)
+        copy = pltpu.make_async_copy(cells_ref.at[cells], out_ref.at[cells], sem.at[b])
         copy.start()
         copies.append(copy)
     for copy in copies:

time: 52.7 us -> 50.3 us (0.954)
  Pallas kernels: 25.7 us -> 23.2 us
    pallas_call x1, Pallas kernels: 23.1 us -> 20.7 us  [patches(): pl.pallas_call(functools.partial(patch_kernel, tiles, slots), out_shape=j...]
where the time goes in v4:
time: 50.3 us; the launch traced here: 50 us
  blocking collectives  26.6 us (53%)
  Pallas kernels  23.2 us (46%)
    all_to_all x1, blocking collectives, per_device(): lax.all_to_all(sent.reshape(sources, used + 2, COLS), ('grid', 'freq'), 0...  26.6 us
    pallas_call x1, Pallas kernels, patches(): pl.pallas_call(functools.partial(patch_kernel, tiles, slots), out_shape=j...  20.7 us
    pallas_call x1, Pallas kernels, per_device(): pl.pallas_call(spectra_kernel, out_shape=jax.ShapeDtypeStruct((tiles, ban...  2.54 us

profile of v4, /device:TPU:0, one launch (start us, length us, event | category | flops | bytes accessed | tf_op | source)
XLA Modules:
  0.0 50.0 jit_solution(9524941790701616270)
XLA Ops:
  0.0 2.5 %spectra.1 = bf16[8,4,82,128]{3,2,1,0:T(8,128)(2,1)} custom-call(bf16[128,2048]{1,0:T(8,128)(2,1)} %bitcast.9, s32[8,16]{1,0:T(8,128)} %bitcast.11, s32[8,16]{1,0:T(8,128)} %bitcast.12), custom_call_target="tpu_custom_call" | custom-call | tf_op jit(solution)/shard_map/spectra/pallas_call | solution.py:574
  2.6 26.6 %all_to_all.5.arrived_ref = bf16[32,82,128]{2,1,0:T(8,128)(2,1)} all-to-all(bf16[32,82,128]{2,1,0:T(8,128)(2,1)} %bitcast.8), channel_id=1, replica_groups=mesh['grid'=8,'freq'=4] {'grid','freq'}, dimensions={0} | all-to-all | bytes 1343488 | tf_op jit(solution)/shard_map/all_to_all | solution.py:590
  29.2 20.7 %patches.1 = f32[192,64,128]{2,1,0:T(8,128)} custom-call(bf16[32,82,128]{2,1,0:T(8,128)(2,1)} %all_to_all.5.arrived_ref, f32[48,64]{1,0:T(8,128)} %bitcast.10), custom_call_target="tpu_custom_call" | custom-call | tf_op jit(solution)/shard_map/patches/pallas_call | solution.py:548

commit v5 on v4

--- a/solution.py
+++ b/solution.py
@@ -195,7 +195,7 @@
     per = min(BLOCK_SRC, sources)
     n = per * slots
     chunks = sources // per
-    members = ((0, 1), (2,), (3, 4))
+    main, rim_tile = (1, 2, 3), (0, None, 4)
     side = chunks + rim_blocks(chunks, n)
     first = (0, side, side + chunks)
 
@@ -228,42 +228,72 @@
             fact = [jnp.where(keep, m + shift + 1.0, 0.0), jnp.where(keep, h + 1.0, 0.0)]
             for ok in inside:
                 fact.append(jnp.zeros_like(h) if ok is None else jnp.where(ok, h + 1.0, 0.0))
-            facts.append(jnp.concatenate(fact + [jnp.zeros((3, n), f32)], 0))
+            facts.append(fact)
             used.append(keep.astype(f32))
-        use = jnp.concatenate(used + [jnp.zeros((8 - SPAN, n), f32)], 0)
+        free = [1.0 - used[1], 1.0 - used[3]]
+        use = jnp.concatenate(used + free + [jnp.zeros((1, n), f32)], 0)
         ranks = dot(use.astype(bf16), before)
         sums = jnp.sum(use, 1, keepdims=True)
-        for k in range(3):
-            for t in members[k]:
-                rank = ranks[t : t + 1] + totals[k]
-                rank_ref[t * chunks + chunk] = jnp.where(use[t : t + 1] > 0.5, rank, -1.0)
-                fact_ref[t * chunks + chunk] = facts[t]
-                totals[k] = totals[k] + sums[t : t + 1]
+        for t in range(SPAN):
+            seat = jnp.zeros((1, n), f32)
+            if t in (1, 3):
+                i = SPAN + t // 2
+                seat = jnp.where(use[i : i + 1] > 0.5, ranks[i : i + 1], -2.0)
+            fact_ref[t * chunks + chunk] = jnp.concatenate(
+                facts[t] + [jnp.zeros((2, n), f32), seat], 0
+            )
+        for i, t in enumerate((0, 4)):
+            rank = ranks[t : t + 1] + totals[i]
+            rank_ref[t * chunks + chunk] = jnp.where(use[t : t + 1] > 0.5, rank, -1.0)
+            totals[i] = totals[i] + sums[t : t + 1]
+            totals[2 + i] = totals[2 + i] + sums[SPAN + i : SPAN + i + 1]
         return tuple(totals)
 
     zero = jnp.zeros((1, 1), f32)
-    totals = over(chunks, locate, (zero, zero, zero))
-    counts = [jnp.max(x).astype(jnp.int32) for x in totals]
-    filled = [(c + (n - 1)) // n for c in counts]
+    totals = over(chunks, locate, (zero,) * 4)
+    seated = totals[2:] if chunks == 1 else (zero, zero)
+    left_over = [
+        jnp.max(jnp.maximum(x - y, 0.0)).astype(jnp.int32) for x, y in zip(totals[:2], seated)
+    ]
+    filled = [
+        chunks + (left_over[0] + (n - 1)) // n,
+        chunks,
+        chunks + (left_over[1] + (n - 1)) // n,
+    ]
 
     p_high, p_low = split(probe_ref[...])
 
-    def pack(k, q):
-        def gather(chunk, total, t):
-            b = t * chunks + chunk
-            wanted = iota((n, n), 0).astype(f32) + (q * n).astype(f32)
-            chosen = (wanted == rank_ref[b]).astype(f32).astype(bf16)
-            values = arrived_ref[pl.ds(chunk * per, per), t * slots : (t + 1) * slots, :]
-            fact = jnp.concatenate([fact_ref[b], jnp.zeros((COLS - 8, n), f32)], 0).T
-            both = jnp.concatenate([values.reshape(n, COLS), fact.astype(bf16)], 1)
-            part = dot(chosen, both)
+    def contents(t, chunk):
+        values = arrived_ref[pl.ds(chunk * per, per), t * slots : (t + 1) * slots, :]
+        fact = jnp.concatenate([fact_ref[t * chunks + chunk], jnp.zeros((COLS - 8, n), f32)], 0)
+        return values.reshape(n, COLS), fact.T
+
+    def moved(chosen, t, chunk):
+        values, fact = contents(t, chunk)
+        both = jnp.concatenate([values, fact.astype(bf16)], 1)
+        return dot(chosen.astype(f32).astype(bf16), both)
+
+    def direct(k, chunk):
+        values, fact = contents(main[k], chunk)
+        total = jnp.concatenate([values.astype(f32), fact], 1)
+        if chunks == 1 and k != 1:
+            guest = moved(fact[:, 7:8] == rank_ref[rim_tile[k]], rim_tile[k], 0)
+            total = jnp.where(fact[:, 0:1] > 0.0, total, guest)
+        finish(first[k] + chunk, total)
+
+    def extra(k, q):
+        wanted = iota((n, n), 0).astype(f32) + ((q - chunks) * n).astype(f32) + seated[k // 2]
+
+        def gather(chunk, total):
+            t = rim_tile[k]
+            part = moved(wanted == rank_ref[t * chunks + chunk], t, chunk)
             return part if total is None else total + part
 
         total = None if chunks == 1 else jnp.zeros((n, 2 * COLS), f32)
-        for t in members[k]:
-            total = over(chunks, functools.partial(gather, t=t), total)
+        finish(first[k] + q, over(chunks, gather, total))
+
+    def finish(b, total):
         flip = total.T
-        b = first[k] + q
         vt_ref[b] = flip[:COLS]
         row, h = flip[COLS : COLS + 1] - 1.0, flip[COLS + 1 : COLS + 2] - 1.0
         column = total[:, COLS : COLS + 8] - 1.0
@@ -280,15 +310,24 @@
         wt_ref[b] = dot(p_high, ohh) + dot(p_low, ohh)
 
     for k in range(3):
-        pack(k, jnp.int32(0))
-
-    for k in range(3):
-
-        def more(q, carry, k=k):
-            pack(k, q)
+
+        def place(chunk, carry, k=k):
+            direct(k, chunk)
             return carry
 
-        lax.fori_loop(1, filled[k], more, 0)
+        over(chunks, place, 0)
+
+    one_block = jnp.maximum(filled[0], filled[2]) <= 1
+
+    @pl.when(jnp.logical_not(one_block))
+    def _():
+        for k in (0, 2):
+
+            def more(q, carry, k=k):
+                extra(k, q)
+                return carry
+
+            lax.fori_loop(chunks, filled[k], more, 0)
 
     st_ref[:, :, RANK:, :] = jnp.zeros((3, JG, RP - RANK, ROWS), f32)
     pp_ref[:, :, RANK:, :] = jnp.zeros((3, FDEV, RP - RANK, COLS), f32)
@@ -367,7 +406,6 @@
                 gram_ref[:, p * (FDEV // 8) + 2 * (g - start) + q2, :] = acc
         return carry
 
-    one_block = jnp.maximum(jnp.maximum(filled[0], filled[1]), filled[2]) <= 1
 
     steps = FDEV // JG
     half = steps // 2

time: 50.3 us -> 49.9 us (level)
  no operation moved by 1% of the time
where the time goes in v5:
time: 49.9 us; the launch traced here: 49.6 us
  blocking collectives  26.6 us (53%)
  Pallas kernels  22.8 us (46%)
    all_to_all x1, blocking collectives, per_device(): lax.all_to_all(sent.reshape(sources, used + 2, COLS), ('grid', 'freq'), 0...  26.6 us
    pallas_call x1, Pallas kernels, patches(): pl.pallas_call(functools.partial(patch_kernel, tiles, slots), out_shape=j...  20.3 us
    pallas_call x1, Pallas kernels, per_device(): pl.pallas_call(spectra_kernel, out_shape=jax.ShapeDtypeStruct((tiles, ban...  2.54 us

profile of v5, /device:TPU:0, one launch (start us, length us, event | category | flops | bytes accessed | tf_op | source)
XLA Modules:
  0.0 49.6 jit_solution(6404040630409515150)
XLA Ops:
  0.0 2.5 %spectra.1 = bf16[8,4,82,128]{3,2,1,0:T(8,128)(2,1)} custom-call(bf16[128,2048]{1,0:T(8,128)(2,1)} %bitcast.9, s32[8,16]{1,0:T(8,128)} %bitcast.11, s32[8,16]{1,0:T(8,128)} %bitcast.12), custom_call_target="tpu_custom_call" | custom-call | tf_op jit(solution)/shard_map/spectra/pallas_call | solution.py:612
  2.6 26.6 %all_to_all.5.arrived_ref = bf16[32,82,128]{2,1,0:T(8,128)(2,1)} all-to-all(bf16[32,82,128]{2,1,0:T(8,128)(2,1)} %bitcast.8), channel_id=1, replica_groups=mesh['grid'=8,'freq'=4] {'grid','freq'}, dimensions={0} | all-to-all | bytes 1343488 | tf_op jit(solution)/shard_map/all_to_all | solution.py:628
  29.2 20.3 %patches.1 = f32[192,64,128]{2,1,0:T(8,128)} custom-call(bf16[32,82,128]{2,1,0:T(8,128)(2,1)} %all_to_all.5.arrived_ref, f32[48,64]{1,0:T(8,128)} %bitcast.10), custom_call_target="tpu_custom_call" | custom-call | tf_op jit(solution)/shard_map/patches/pallas_call | solution.py:586

commit v6 on v5

--- a/solution.py
+++ b/solution.py
@@ -521,8 +521,15 @@
                 c = pp_ref[p, pl.ds(i * 4, 4)].reshape(wide, COLS)
                 if p == 1:
                     p_high, p_low = split(c)
-                    twice = dot(b_high, jnp.concatenate([p_high, p_low], 1))
-                    c = twice[:, :COLS] + twice[:, COLS:] + dot(b_low, p_high)
+                    terms = jnp.concatenate(
+                        [
+                            jnp.concatenate([p_high, p_low], 1),
+                            jnp.concatenate([p_high, jnp.zeros_like(p_low)], 1),
+                        ],
+                        0,
+                    )
+                    twice = dot(jnp.concatenate([b_high, b_low], 1), terms)
+                    c = twice[:, :COLS] + twice[:, COLS:]
                 else:
                     edge_rows = pl.ds(0 if p == 0 else OWN_ROWS - RIM, RIM)
                     x = own_ref[i, edge_rows, :].astype(bf16)

time: 49.9 us -> 49.8 us (level)
  no operation moved by 1% of the time
where the time goes in v6:
time: 49.8 us; the launch traced here: 49.6 us
  blocking collectives  26.6 us (53%)
  Pallas kernels  22.8 us (46%)
    all_to_all x1, blocking collectives, per_device(): lax.all_to_all(sent.reshape(sources, used + 2, COLS), ('grid', 'freq'), 0...  26.6 us
    pallas_call x1, Pallas kernels, patches(): pl.pallas_call(functools.partial(patch_kernel, tiles, slots), out_shape=j...  20.2 us
    pallas_call x1, Pallas kernels, per_device(): pl.pallas_call(spectra_kernel, out_shape=jax.ShapeDtypeStruct((tiles, ban...  2.54 us

profile of v6, /device:TPU:0, one launch (start us, length us, event | category | flops | bytes accessed | tf_op | source)
XLA Modules:
  0.0 49.6 jit_solution(11817648789735542083)
XLA Ops:
  0.0 2.5 %spectra.1 = bf16[8,4,82,128]{3,2,1,0:T(8,128)(2,1)} custom-call(bf16[128,2048]{1,0:T(8,128)(2,1)} %bitcast.9, s32[8,16]{1,0:T(8,128)} %bitcast.11, s32[8,16]{1,0:T(8,128)} %bitcast.12), custom_call_target="tpu_custom_call" | custom-call | tf_op jit(solution)/shard_map/spectra/pallas_call | solution.py:619
  2.6 26.6 %all_to_all.5.arrived_ref = bf16[32,82,128]{2,1,0:T(8,128)(2,1)} all-to-all(bf16[32,82,128]{2,1,0:T(8,128)(2,1)} %bitcast.8), channel_id=1, replica_groups=mesh['grid'=8,'freq'=4] {'grid','freq'}, dimensions={0} | all-to-all | bytes 1343488 | tf_op jit(solution)/shard_map/all_to_all | solution.py:635
  29.2 20.2 %patches.1 = f32[192,64,128]{2,1,0:T(8,128)} custom-call(bf16[32,82,128]{2,1,0:T(8,128)(2,1)} %all_to_all.5.arrived_ref, f32[48,64]{1,0:T(8,128)} %bitcast.10), custom_call_target="tpu_custom_call" | custom-call | tf_op jit(solution)/shard_map/patches/pallas_call | solution.py:593
